TPU v7x, 256 devices: a whole 4x4x8 slice. The times are simulated.
256 devices in a mesh: tok: 8 (over z), ch: 32 (over y, x, core).
Axes of the slice: x: 4, y: 4, z: 8, core: 2. Of those that a mesh axis runs over, the one named last changes fastest.
Arguments:
- tokens: bfloat16 [16384, 1024], P('tok', 'ch'), may hold values from -6 to 6
- filter_in: float32 [2, 8, 128, 128], replicated, may hold values from -0.375 to 0.375
- filter_out: float32 [2, 8, 128, 128], replicated, may hold values from -0.375 to 0.375
- up_weight: bfloat16 [1024, 4096], P('ch', 'tok'), may hold values from -0.1875 to 0.1875
- down_weight: bfloat16 [4096, 1024], P('tok', 'ch'), may hold values from -0.09375 to 0.09375
- cotangent: bfloat16 [16384, 1024], P('tok', 'ch'), may hold values from -6 to 6
Outputs:
- mixed: bfloat16 [16384, 1024], P('tok', 'ch')
- grad_tokens: bfloat16 [16384, 1024], P('tok', 'ch')
- grad_up: float32 [1024, 4096], P('ch', 'tok')
- grad_down: float32 [4096, 1024], P('tok', 'ch')
- grad_filter_in: float32 [2, 8, 128, 128], replicated
- grad_filter_out: float32 [2, 8, 128, 128], replicated
All inputs are finite; a program needn't handle non-finite values.
Results may differ from a plain program's by a relative error of at most 0.02.
Values may be sent and summed in bfloat16 or wider, within the bound.
A program may use at most 128 MiB of HBM per device.

v0:
```python
import math

import jax
import jax.numpy as jnp
from jax import lax
from jax.sharding import PartitionSpec as P

NX = 32
NY = 64
NZ = 8


highest = lax.Precision.HIGHEST


def gelu_tanh(values):
    return jax.nn.gelu(values, approximate=True)


def phase_table(length):
    counter = jnp.arange(length, dtype=jnp.int32)
    turns = (counter[:, None] * counter[None, :] % length).astype(jnp.float32)
    angle = 2.0 * math.pi / length * turns
    factor = 1.0 / math.sqrt(length)
    return (jnp.cos(angle) * factor, jnp.sin(angle) * factor)


def plane_table():
    counter = jnp.arange(NY * NZ, dtype=jnp.int32)
    row_index = counter // NZ
    col_index = counter % NZ
    row_turns = (row_index[:, None] * row_index[None, :] % NY).astype(jnp.float32) / NY
    col_turns = (col_index[:, None] * col_index[None, :] % NZ).astype(jnp.float32) / NZ
    angle = 2.0 * math.pi * (row_turns + col_turns)
    factor = 1.0 / math.sqrt(NY * NZ)
    return (jnp.cos(angle) * factor, jnp.sin(angle) * factor)


def plane_forward(slab, cosine, sine):
    real_part = jnp.einsum("qp,apc->aqc", cosine, slab, precision=highest)
    imag_part = -jnp.einsum("qp,apc->aqc", sine, slab, precision=highest)
    return jnp.stack([real_part, imag_part])


def plane_inverse(spectrum, cosine, sine):
    first = jnp.einsum("qp,apc->aqc", cosine, spectrum[0], precision=highest)
    second = jnp.einsum("qp,apc->aqc", sine, spectrum[1], precision=highest)
    return first - second


def line_transform(spectrum, cosine, sine, direction):

    def contract_rows(table, values):
        return jnp.einsum("kn,nqc->kqc", table, values, precision=highest)

    real_part = contract_rows(cosine, spectrum[0]) + direction * contract_rows(sine, spectrum[1])
    imag_part = contract_rows(cosine, spectrum[1]) - direction * contract_rows(sine, spectrum[0])
    return jnp.stack([real_part, imag_part])


def complex_layer(real_part, imag_part, weight):

    def contract(values, matrix):
        return jnp.einsum("kqnb,nbd->kqnd", values, matrix, precision=highest)

    first = contract(real_part, weight[0]) - contract(imag_part, weight[1])
    second = contract(real_part, weight[1]) + contract(imag_part, weight[0])
    return (first, second)


def channel_mixing(pencil, filter_in, filter_out):
    blocks = filter_in.shape[1]
    shaped = pencil.reshape(2, pencil.shape[1], pencil.shape[2], blocks, pencil.shape[3] // blocks)
    first_real, first_imag = complex_layer(shaped[0], shaped[1], filter_in)
    second_real, second_imag = complex_layer(
        gelu_tanh(first_real), gelu_tanh(first_imag), filter_out
    )
    return jnp.stack([second_real, second_imag]).reshape(pencil.shape)


def lines_out(spectrum):
    return lax.all_to_all(spectrum, "tok", split_axis=2, concat_axis=1, tiled=True)


def lines_back(spectrum):
    return lax.all_to_all(spectrum, "tok", split_axis=1, concat_axis=2, tiled=True)


def channels_out(spectrum):
    return lax.all_to_all(spectrum, "ch", split_axis=2, concat_axis=3, tiled=True)


def channels_back(spectrum):
    return lax.all_to_all(spectrum, "ch", split_axis=3, concat_axis=2, tiled=True)


def token_group(values):
    blocks = lax.all_to_all(values, "ch", split_axis=0, concat_axis=1, tiled=True)
    return lax.all_gather(blocks, "tok", axis=0, tiled=True)


def contract_first(left, right):
    return lax.dot_general(
        left, right, (((0,), (0,)), ((), ())), preferred_element_type=jnp.float32
    )


def contract_last(left, right):
    return lax.dot_general(
        left, right, (((1,), (1,)), ((), ())), preferred_element_type=jnp.float32
    )


def local(tokens, filter_in, filter_out, up_weight, down_weight, cotangent):
    rows, local_width = tokens.shape
    planes = rows // (NY * NZ)
    plane_cos, plane_sin = plane_table()
    line_cos, line_sin = phase_table(NX)
    signal = tokens.astype(jnp.float32).reshape(planes, NY * NZ, local_width)
    slab_spec, forward_vjp = jax.vjp(
        lambda values: plane_forward(values, plane_cos, plane_sin), signal
    )
    first_lines = lines_out(slab_spec)
    turned, turn_vjp = jax.vjp(
        lambda values: line_transform(values, line_cos, line_sin, 1.0), first_lines
    )
    pencil = channels_out(turned)
    filtered, mix_vjp = jax.vjp(channel_mixing, pencil, filter_in, filter_out)
    back_lines = channels_back(filtered)
    returned, return_vjp = jax.vjp(
        lambda values: line_transform(values, line_cos, line_sin, -1.0), back_lines
    )
    back_slab = lines_back(returned)
    branch, inverse_vjp = jax.vjp(
        lambda values: plane_inverse(values, plane_cos, plane_sin), back_slab
    )
    middle = (signal + branch).reshape(rows, local_width).astype(jnp.bfloat16)
    up_columns, down_rows = (
        lax.all_gather(up_weight, "ch", axis=0, tiled=True),
        lax.all_gather(down_weight, "ch", axis=1, tiled=True),
    )
    middle_rows = token_group(middle)
    pre_hidden = jnp.dot(middle_rows, up_columns, preferred_element_type=jnp.float32)
    activated, gelu_vjp = jax.vjp(gelu_tanh, pre_hidden)
    hidden = activated.astype(jnp.bfloat16)
    piece = hidden
    projected_share = lax.psum_scatter(
        jnp.dot(piece, down_rows, preferred_element_type=jnp.float32).astype(jnp.bfloat16),
        "tok",
        scatter_dimension=0,
        tiled=True,
    ).astype(jnp.float32)
    projected = lax.all_to_all(
        projected_share.astype(jnp.bfloat16), "ch", split_axis=1, concat_axis=0, tiled=True
    ).astype(projected_share.dtype)
    mixed = (middle.astype(jnp.float32) + projected).astype(jnp.bfloat16)
    cotangent_rows = token_group(cotangent)
    back_hidden = contract_last(cotangent_rows, down_rows)
    down_term = contract_first(hidden, cotangent_rows)
    grad_down = lax.psum_scatter(
        down_term.astype(jnp.bfloat16), "ch", scatter_dimension=1, tiled=True
    ).astype(jnp.float32)
    grad_pre = gelu_vjp(back_hidden)[0].astype(jnp.bfloat16)
    up_term = contract_first(middle_rows, grad_pre)
    grad_up = lax.psum_scatter(
        up_term.astype(jnp.bfloat16), "ch", scatter_dimension=0, tiled=True
    ).astype(jnp.float32)
    piece = grad_pre
    input_share = lax.psum_scatter(
        contract_last(piece, up_columns).astype(jnp.bfloat16),
        "tok",
        scatter_dimension=0,
        tiled=True,
    ).astype(jnp.float32)
    input_term = lax.all_to_all(
        input_share.astype(jnp.bfloat16), "ch", split_axis=1, concat_axis=0, tiled=True
    ).astype(input_share.dtype)
    grad_middle = cotangent.astype(jnp.float32) + input_term
    grad_back_slab = inverse_vjp(grad_middle.reshape(planes, NY * NZ, local_width))[0]
    grad_back_lines = return_vjp(lines_out(grad_back_slab))[0]
    grad_pencil, grad_first, grad_second = mix_vjp(channels_out(grad_back_lines))
    grad_slab = lines_back(turn_vjp(channels_back(grad_pencil))[0])
    grad_filter_in, grad_filter_out = lax.psum((grad_first, grad_second), ("tok", "ch"))
    spectral_grad = forward_vjp(grad_slab)[0].reshape(rows, local_width)
    grad_tokens = (grad_middle + spectral_grad).astype(jnp.bfloat16)
    return (mixed, grad_tokens, grad_up, grad_down, grad_filter_in, grad_filter_out)


def solution(mesh):
    in_specs = (P("tok", "ch"), P(), P(), P("ch", "tok"), P("tok", "ch"), P("tok", "ch"))
    out_specs = (P("tok", "ch"), P("tok", "ch"), P("ch", "tok"), P("tok", "ch"), P(), P())
    return jax.shard_map(local, mesh=mesh, in_specs=in_specs, out_specs=out_specs, check_vma=False)
```

profile of v0, /device:TPU:1, one launch (start us, length us, event | category | flops | bytes accessed | tf_op | source)
XLA Modules:
  0.0 923.2 jit_solution(3735122529022306470)
XLA Ops:
  9.3 8.6 all-to-all-start.6
  18.8 5.2 fusion.40
  24.0 5.2 fusion.39
  32.7 8.2 all-to-all-start
  42.0 16.9 %all-to-all-done = f32[8,1,16384]{2,1,0:T(1,128)S(1)} async-done(((f32[8,1,16384]{2,1,0:T(1,128)}), f32[8,1,16384]{2,1,0:T(1,128)S(1)}, u32[]{:S(2)}, u32[]{:S(2)}) %all-to-all-start) | async-done | bytes 524320 | tf_op jit(solution)/shard_map/all_to_all | solution.py:82
  70.6 7.5 all-to-all-start.1
  78.9 10.8 %all-to-all-done.1 = f32[32,1,4096]{2,1,0:T(1,128)S(1)} async-done(((f32[32,1,4096]{2,1,0:T(1,128)}), f32[32,1,4096]{2,1,0:T(1,128)S(1)}, u32[]{:S(2)}, u32[]{:S(2)}) %all-to-all-start.1) | async-done | bytes 524320 | tf_op jit(solution)/shard_map/all_to_all | solution.py:90
  112.9 4.3 reshape.176
  117.2 4.7 all-to-all-start.2
  123.1 11.5 %all-to-all-done.2 = f32[32,1,4096]{2,1,0:T(1,128)} async-done(((f32[32,1,4096]{2,1,0:T(1,128)}), f32[32,1,4096]{2,1,0:T(1,128)}, u32[]{:S(2)}, u32[]{:S(2)}) %all-to-all-start.2) | async-done | bytes 524320 | tf_op jit(solution)/shard_map/all_to_all | solution.py:94
  142.4 4.3 copy.247
  170.6 20.6 %all_to_all.181 = f32[8,1,16384]{2,1,0:T(1,128)} all-to-all(f32[8,1,16384]{2,1,0:T(1,128)} %reshape.178), channel_id=1, replica_groups=mesh['tok'=8,'ch'=32] {'tok'}, dimensions={0} | all-to-all | bytes 1048576 | tf_op jit(solution)/shard_map/all_to_all | solution.py:86
  203.2 6.6 fusion.37
  209.8 5.9 fusion.15
  218.6 13.3 %all_to_all.182 = bf16[32,2,1024]{2,1,0:T(2,128)(2,1)S(1)} all-to-all(bf16[32,2,1024]{2,1,0:T(2,128)(2,1)S(1)} %reshape.180), channel_id=1, replica_groups=mesh['tok'=8,'ch'=32] {'ch'}, dimensions={0} | all-to-all | bytes 262144 | tf_op jit(solution)/shard_map/all_to_all | solution.py:98
  236.3 22.9 %all-gather.5.cloned.1.call-done = bf16[512,1024]{1,0:T(8,128)(2,1)} async-done(((bf16[64,1024]{1,0:T(8,128)(2,1)}), bf16[512,1024]{1,0:T(8,128)(2,1)}) %all-gather.5.cloned.1.call-update) | async-done | bytes 1048592 | tf_op jit(solution)/shard_map/all_gather | solution.py:99
  272.5 30.9 %reduce-scatter.7.cloned.1.call-done = bf16[64,1024]{1,0:T(8,128)(2,1)} async-done(((bf16[512,1024]{1,0:T(8,128)(2,1)}), bf16[64,1024]{1,0:T(8,128)(2,1)}) %reduce-scatter.7.cloned.1.call-update) | async-done | bytes 131088 | tf_op jit(solution)/shard_map/reduce_scatter | solution.py:169
  305.3 12.5 %all-to-all-start.7 = ((bf16[32,2,1024]{2,1,0:T(2,128)(2,1)}), bf16[32,2,1024]{2,1,0:T(2,128)(2,1)}, u32[]{:S(2)}, u32[]{:S(2)}) async-start(bf16[32,2,1024]{2,1,0:T(2,128)(2,1)} %reshape.186), calls=%async_computation.9 | async-start | bytes 262144 | tf_op jit(solution)/shard_map/all_to_all | solution.py:175
  321.3 23.2 %reduce-scatter.5.cloned.1.call-done = bf16[64,1024]{1,0:T(8,128)(2,1)} async-done(((bf16[512,1024]{1,0:T(8,128)(2,1)}), bf16[64,1024]{1,0:T(8,128)(2,1)}) %reduce-scatter.5.cloned.1.call-update) | async-done | bytes 131088 | tf_op jit(solution)/shard_map/reduce_scatter | solution.py:147
  346.4 11.8 %all-to-all-start.5 = ((bf16[32,2,1024]{2,1,0:T(2,128)(2,1)}), bf16[32,2,1024]{2,1,0:T(2,128)(2,1)}, u32[]{:S(2)}, u32[]{:S(2)}) async-start(bf16[32,2,1024]{2,1,0:T(2,128)(2,1)} %reshape.182), calls=%async_computation.6 | async-start | bytes 262144 | tf_op jit(solution)/shard_map/all_to_all | solution.py:153
  361.8 5.3 convolution_bitcast_fusion.17
  367.1 5.2 convolution_bitcast_fusion.16
  384.5 50.3 %reduce-scatter.9.cloned.1.call-done = bf16[32,512]{1,0:T(8,128)(2,1)} async-done(((bf16[1024,512]{1,0:T(8,128)(2,1)}), bf16[32,512]{1,0:T(8,128)(2,1)}) %reduce-scatter.9.cloned.1.call-update) | async-done | bytes 32784 | tf_op jit(solution)/shard_map/reduce_scatter | solution.py:165
  436.2 87.4 %reduce-scatter.11.cloned.1.call-done = bf16[512,32]{0,1:T(8,128)(2,1)} async-done(((bf16[512,1024]{0,1:T(8,128)(2,1)}), bf16[512,32]{0,1:T(8,128)(2,1)}) %reduce-scatter.11.cloned.1.call-update) | async-done | bytes 32784 | tf_op jit(solution)/shard_map/reduce_scatter | solution.py:160
  548.5 7.3 all-to-all-start.9
  559.9 7.6 all-to-all-done.9
  615.8 6.2 all-to-all-done.10
  640.5 6.9 all-to-all-start.11
  654.3 11.1 %all-to-all-done.11 = f32[8,1,16384]{2,1,0:T(1,128)S(1)} async-done(((f32[8,1,16384]{2,1,0:T(1,128)}), f32[8,1,16384]{2,1,0:T(1,128)S(1)}, u32[]{:S(2)}, u32[]{:S(2)}) %all-to-all-start.11) | async-done | bytes 524320 | tf_op jit(solution)/shard_map/all_to_all | solution.py:86
  668.6 5.3 fusion.31
  673.9 5.5 fusion.12
  680.1 232.8 %all-reduce.23.cloned.1.call-done = (f32[2,8,128,128]{3,2,1,0:T(8,128)}, f32[2,8,128,128]{3,2,1,0:T(8,128)}) async-done(((f32[2,8,128,128]{3,2,1,0:T(8,128)}, f32[2,8,128,128]{3,2,1,0:T(8,128)}), (f32[2,8,128,128]{3,2,1,0:T(8,128)}, f32[2,8,128,128]{3,2,1,0:T(8,128)})) %all-reduce.23.cloned.1.call-update) | async-done | bytes 2097168 | tf_op jit(solution)/shard_map/psum | solution.py:183
  (234 shorter events, 242.5 us)
Async XLA Ops:
  9.3 23.4 %all-to-all-start.6 = ((bf16[32,2,1024]{2,1,0:T(2,128)(2,1)}), bf16[32,2,1024]{2,1,0:T(2,128)(2,1)S(1)}, u32[]{:S(2)}, u32[]{:S(2)}) async-start(bf16[32,2,1024]{2,1,0:T(2,128)(2,1)} %reshape.184), calls=%async_computation.7 | async-start | bytes 262144 | tf_op jit(solution)/shard_map/all_to_all | solution.py:98
  32.7 26.1 %all-to-all-start = ((f32[8,1,16384]{2,1,0:T(1,128)}), f32[8,1,16384]{2,1,0:T(1,128)S(1)}, u32[]{:S(2)}, u32[]{:S(2)}) async-start(f32[8,1,16384]{2,1,0:T(1,128)} %reshape.172), calls=%async_computation | async-start | bytes 1048576 | tf_op jit(solution)/shard_map/all_to_all | solution.py:82
  40.9 192.2 %all-gather.11.cloned.1.call-start = ((), (), s32[]{:S(2)}) async-start(), calls=%async_computation.20 | async-start | bytes 1179648 | tf_op jit(solution)/shard_map/all_gather | solution.py:99
  70.6 19.1 %all-to-all-start.1 = ((f32[32,1,4096]{2,1,0:T(1,128)}), f32[32,1,4096]{2,1,0:T(1,128)S(1)}, u32[]{:S(2)}, u32[]{:S(2)}) async-start(f32[32,1,4096]{2,1,0:T(1,128)} %reshape.174), calls=%async_computation.1 | async-start | bytes 1048576 | tf_op jit(solution)/shard_map/all_to_all | solution.py:90
  78.1 155.0 %all-gather.9.cloned.1.call-start = ((), (), s32[]{:S(2)}) async-start(), calls=%async_computation.18 | async-start | bytes 1081344 | tf_op jit(solution)/shard_map/all_gather | solution.py:140
  117.2 17.3 %all-to-all-start.2 = ((f32[32,1,4096]{2,1,0:T(1,128)}), f32[32,1,4096]{2,1,0:T(1,128)}, u32[]{:S(2)}, u32[]{:S(2)}) async-start(f32[32,1,4096]{2,1,0:T(1,128)} %reshape.176), calls=%async_computation.2 | async-start | bytes 1048576 | tf_op jit(solution)/shard_map/all_to_all | solution.py:94
  121.9 114.5 %all-gather.7.cloned.1.call-start = ((), (), s32[]{:S(2)}) async-start(), calls=%async_computation.17 | async-start | bytes 1081344 | tf_op jit(solution)/shard_map/all_gather | solution.py:139
  122.6 136.6 %all-gather.5.cloned.1.call-start = ((), (), s32[]{:S(2)}) async-start(), calls=%async_computation.16 | async-start | bytes 1179648 | tf_op jit(solution)/shard_map/all_gather | solution.py:99
  161.7 3.7 copy-start.2
  203.2 6.6 copy-start.19
  233.0 70.3 %reduce-scatter.7.cloned.1.call-start = ((), (), s32[]{:S(2)}) async-start(), calls=%async_computation.21 | async-start | bytes 1179648 | tf_op jit(solution)/shard_map/reduce_scatter | solution.py:169
  259.2 4.9 copy-start.20
  265.9 78.6 %reduce-scatter.5.cloned.1.call-start = ((), (), s32[]{:S(2)}) async-start(), calls=%async_computation.19 | async-start | bytes 1179648 | tf_op jit(solution)/shard_map/reduce_scatter | solution.py:147
  269.3 165.5 %reduce-scatter.9.cloned.1.call-start = ((), (), s32[]{:S(2)}) async-start(), calls=%async_computation.22 | async-start | bytes 1081344 | tf_op jit(solution)/shard_map/reduce_scatter | solution.py:165
  305.3 41.2 %all-to-all-start.7 = ((bf16[32,2,1024]{2,1,0:T(2,128)(2,1)}), bf16[32,2,1024]{2,1,0:T(2,128)(2,1)}, u32[]{:S(2)}, u32[]{:S(2)}) async-start(bf16[32,2,1024]{2,1,0:T(2,128)(2,1)} %reshape.186), calls=%async_computation.9 | async-start | bytes 262144 | tf_op jit(solution)/shard_map/all_to_all | solution.py:175
  317.8 205.8 %reduce-scatter.11.cloned.1.call-start = ((), (), s32[]{:S(2)}) async-start(), calls=%async_computation.23 | async-start | bytes 1081344 | tf_op jit(solution)/shard_map/reduce_scatter | solution.py:160
  321.3 40.5 %copy-start.16 = (bf16[2048,32]{0,1:T(8,128)(2,1)S(1)}, bf16[2048,32]{0,1:T(8,128)(2,1)}, u32[]{:S(2)}) copy-start(bf16[2048,32]{0,1:T(8,128)(2,1)} %param.11) | copy-start | bytes 393220
  346.4 33.0 %all-to-all-start.5 = ((bf16[32,2,1024]{2,1,0:T(2,128)(2,1)}), bf16[32,2,1024]{2,1,0:T(2,128)(2,1)}, u32[]{:S(2)}, u32[]{:S(2)}) async-start(bf16[32,2,1024]{2,1,0:T(2,128)(2,1)} %reshape.182), calls=%async_computation.6 | async-start | bytes 262144 | tf_op jit(solution)/shard_map/all_to_all | solution.py:153
  361.8 5.3 copy-start.14
  375.8 7.9 copy-start.18
  379.5 146.6 %all-to-all-start.8 = ((f32[8,1,16384]{2,1,0:T(1,128)}), f32[8,1,16384]{2,1,0:T(1,128)}, u32[]{:S(2)}, u32[]{:S(2)}) async-start(f32[8,1,16384]{2,1,0:T(1,128)} %reshape.188), calls=%async_computation.10 | async-start | bytes 1048576 | tf_op jit(solution)/shard_map/all_to_all | solution.py:82
  548.5 19.0 %all-to-all-start.9 = ((f32[32,1,4096]{2,1,0:T(1,128)}), f32[32,1,4096]{2,1,0:T(1,128)}, u32[]{:S(2)}, u32[]{:S(2)}) async-start(f32[32,1,4096]{2,1,0:T(1,128)} %reshape.190), calls=%async_computation.11 | async-start | bytes 1048576 | tf_op jit(solution)/shard_map/all_to_all | solution.py:90
  583.3 3.7 copy-start.9
  583.3 3.7 copy-start.5
  606.2 7.8 copy-start.7
  606.2 15.8 %all-to-all-start.10 = ((f32[32,1,4096]{2,1,0:T(1,128)}), f32[32,1,4096]{2,1,0:T(1,128)S(1)}, u32[]{:S(2)}, u32[]{:S(2)}) async-start(f32[32,1,4096]{2,1,0:T(1,128)} %reshape.192), calls=%async_computation.12 | async-start | bytes 1048576 | tf_op jit(solution)/shard_map/all_to_all | solution.py:94
  638.4 9.3 %copy-start.11 = (f32[1,8,128,128]{3,2,1,0:T(8,128)S(1)}, f32[1,8,128,128]{3,2,1,0:T(8,128)}, u32[]{:S(2)}) copy-start(f32[1,8,128,128]{3,2,1,0:T(8,128)} %convolution_bitcast_fusion) | copy-start | bytes 1572868
  640.5 9.6 %copy-start.4 = (f32[8,128,32,2]{1,2,3,0:T(8,128)S(1)}, f32[8,128,32,2]{1,2,3,0:T(8,128)}, u32[]{:S(2)}) copy-start(f32[8,128,32,2]{1,2,3,0:T(8,128)} %copy-done.3) | copy-start | bytes 786436
  640.5 24.8 %all-to-all-start.11 = ((f32[8,1,16384]{2,1,0:T(1,128)}), f32[8,1,16384]{2,1,0:T(1,128)S(1)}, u32[]{:S(2)}, u32[]{:S(2)}) async-start(f32[8,1,16384]{2,1,0:T(1,128)} %reshape.194), calls=%async_computation.13 | async-start | bytes 1048576 | tf_op jit(solution)/shard_map/all_to_all | solution.py:86
  647.4 4.8 copy-start.8
  647.4 265.5 %all-reduce.23.cloned.1.call-start = ((), (), s32[]{:S(2)}) async-start(), calls=%async_computation.24 | async-start | bytes 4194304 | tf_op jit(solution)/shard_map/psum | solution.py:183
  673.9 5.5 copy-start.15
  (9 other events, 19.6 us)
Sparse Core Ops, SparseCore 0:
  44.1 35.2 all-gather.10
  81.9 53.9 all-gather.8
  138.5 46.7 all-gather.6
  233.1 26.0 all-gather.4
  266.0 37.2 reduce-scatter.6
  306.3 38.1 reduce-scatter.4
  348.3 86.4 reduce-scatter.8
  439.0 84.4 reduce-scatter.10
  654.4 258.4 all-reduce.22
where the time goes:
time: 936 us; the launch traced here: 923 us
  waiting for transfers between devices  513 us (55%)
  local copies, waits for them, and re-layouts  143 us (15%)
  matrix products  104 us (11%)
  starting transfers between devices  76.8 us (8%)
  other arithmetic  36.4 us (4%)
  blocking collectives  33.9 us (4%)
  between operations  15.3 us (2%)
    psum x1, waiting for transfers between devices, local(): lax.psum((grad_first, grad_second), ('tok', 'ch'))  233 us
    reduce_scatter x1, waiting for transfers between devices, local(): lax.psum_scatter(down_term.astype(jnp.bfloat16), 'ch', scatter_dimension=...  87.4 us
    reduce_scatter x1, waiting for transfers between devices, local(): lax.psum_scatter(up_term.astype(jnp.bfloat16), 'ch', scatter_dimension=0,...  50.3 us
    unnamed x70, local copies, waits for them, and re-layouts  50.3 us
    reduce_scatter x1, waiting for transfers between devices, local(): lax.psum_scatter(contract_last(piece, up_columns).astype(jnp.bfloat16), '...  30.9 us
    dot_general x24, matrix products, contract(): return jnp.einsum('kqnb,nbd->kqnd', values, matrix, precision=highest)  26.5 us
    reduce_scatter x1, waiting for transfers between devices, local(): lax.psum_scatter(jnp.dot(piece, down_rows, preferred_element_type=jnp.flo...  23.2 us
    all_gather x2, waiting for transfers between devices, token_group(): return lax.all_gather(blocks, 'tok', axis=0, tiled=True)  22.9 us
  transfers between devices with their start and end apart: 19, of which 12 were waited for; matrix products, arithmetic and copies ran while one was open for 21% of the time, Pallas kernels for 0%

commit v1 on v0

v1 whole, which is shorter than its diff:
```python
import functools
import math

import jax
import jax.numpy as jnp
import ml_dtypes
import numpy as np
from jax import lax
from jax.experimental import pallas as pl
from jax.experimental.pallas import tpu as pltpu
from jax.sharding import PartitionSpec as P

NY = 64
NZ = 8
QG = 4
STRIDE = 11
LANES = 128

f32 = jnp.float32
bf16 = jnp.bfloat16
HIGHEST = lax.Precision.HIGHEST
MESH = pl.DeviceIdType.MESH


@functools.lru_cache(None)
def tables(nz, planes):
    groups = nz * QG
    nx = nz * planes
    plane = NY * NZ
    singles = [(0, 0), (0, NZ // 2), (NY // 2, 0), (NY // 2, NZ // 2)]
    pairs = []
    for v in range(NY):
        for w in range(NZ):
            other = ((-v) % NY, (-w) % NZ)
            if (v, w) < other:
                pairs.append((v, w))
    j = np.repeat(np.arange(NY), NZ)
    k = np.tile(np.arange(NZ), NY)
    rows = []
    for v, w in singles:
        rows.append(np.cos(2 * np.pi * (v * j / NY + w * k / NZ)))
    for v, w in pairs:
        angle = 2 * np.pi * (((v * j) % NY) / NY + ((w * k) % NZ) / NZ)
        rows.append(np.cos(angle))
        rows.append(-np.sin(angle))
    full = np.stack(rows) / math.sqrt(plane)
    assert full.shape == (plane, plane)
    high = full.astype(ml_dtypes.bfloat16)
    low = (full - high.astype(np.float64)).astype(ml_dtypes.bfloat16)
    u = np.arange(nx)
    turn = 2 * np.pi * ((u[:, None] * u[None, :]) % nx) / nx
    cos, sin = np.cos(turn) / math.sqrt(nx), np.sin(turn) / math.sqrt(nx)
    pair = np.zeros((2, nx, 2, 2, nx))
    pair[0, :, 0, 0], pair[0, :, 0, 1] = cos, sin
    pair[1, :, 0, 0], pair[1, :, 0, 1] = -sin, cos
    pair[0, :, 1, 0], pair[0, :, 1, 1] = cos, sin
    pair[1, :, 1, 0], pair[1, :, 1, 1] = sin, -cos
    two = np.zeros((2, nx, 2, 2, nx))
    two[0, :, 0, 0], two[1, :, 0, 0] = cos, -sin
    two[0, :, 1, 1], two[1, :, 1, 1] = cos, -sin

    def ordered(table):
        table = table.reshape(4 * nx, 2, nz, planes).transpose(0, 3, 1, 2)
        return table.reshape(4 * nx, 2 * nx).astype(np.float32)

    width = LANES // QG
    lane = np.zeros((QG * LANES, QG * LANES), np.float32)
    for q in range(QG):
        for i in range(planes):
            for c in range(width):
                lane[q * LANES + i * width + c, i * LANES + q * width + c] = 1.0
    comps = plane // groups
    row = np.zeros((nz * comps, nz * comps), np.float32)
    for z in range(nz):
        for r in range(comps):
            row[r * nz + z, z * comps + r] = 1.0
    return dict(
        high=high,
        low=low,
        pair=ordered(pair),
        two=ordered(two),
        lane=lane.astype(ml_dtypes.bfloat16),
        row=row.astype(ml_dtypes.bfloat16),
    )


def dot(a, b, ca=1, cb=0, precision=None):
    return lax.dot_general(
        a, b, (((ca,), (cb,)), ((), ())), precision=precision, preferred_element_type=f32
    )


SCALE = math.sqrt(2.0 / math.pi)
CUBIC = 0.044715


def gelu(x):
    t = jnp.tanh(SCALE * (x + CUBIC * (x * x * x)))
    return 0.5 * x * (1.0 + t)


def gelu_slope(x):
    t = jnp.tanh(SCALE * (x + CUBIC * (x * x * x)))
    return 0.5 * (1.0 + t) + 0.5 * x * (1.0 - t * t) * (SCALE * (1.0 + 3.0 * CUBIC * (x * x)))


def split(x):
    high = x.astype(bf16)
    return high, (x - high.astype(f32)).astype(bf16)


def kernel(
    nz, nc, planes,
    tokens_in, cotangent_in, up_in, down_in, filter_in, filter_out,
    plh_in, pll_in, mg_in, mt_in, lane_in, row_in,
    mixed, gtok, gup, gdn, gfi, gfo,
    a1s, a1r, a2s, a2r, a3s, a3r, a4s, a4r,
    xs, as_, fil, toks_t, cts, wts,
    mid, midg, cotg, wb, back, hid, gpre,
    gms, gmx, gmh, gmr, prs, prx, prh, prr, gw, gr1, gs, gr2,
    gfs, gfr, gfp, gfz, gfall,
    tokens, cotangent, plh, pll, mg, mt, lane, row,
    send, recv, local,
):
    ny = planes
    nh = nc // ny
    ng = nz * QG
    nb = nc // QG
    nx = nz * planes
    comps = a1s.shape[1]
    cols = comps // 2
    width, plane = wts.shape[1], mid.shape[3]
    hidden = hid.shape[0]
    z = lax.axis_index("tok")
    c = lax.axis_index("ch")
    y, h = c // nh, lax.rem(c, nh)
    b, q = c // QG, lax.rem(c, QG)
    d = z * QG + q
    core = lax.rem(c, 2)
    other = 1 - core
    sibling = c + 1 - 2 * core

    def remote(src, dst, phase, zz, cc):
        pltpu.make_async_remote_copy(
            src_ref=src, dst_ref=dst, send_sem=send.at[phase], recv_sem=recv.at[phase],
            device_id=(zz, cc), device_id_type=MESH,
        ).start()

    def here(src, dst, phase):
        pltpu.make_async_copy(src, dst, recv.at[phase]).start()

    def wait(ref, sems, phase):
        pltpu.make_async_copy(ref, ref, sems.at[phase]).wait()

    near = pl.ds(0, nc - 1)
    quarter = wb.at[0, pl.ds(0, nh)]
    small = a1s.at[pl.ds(0, ng - 1)]
    filters = gfr.at[pl.ds(0, ng - 1)]
    half = nz // 2
    brings = {
        0: a1r, 1: a2r, 2: a3r, 3: a4r, 4: quarter, 23: quarter, 5: cotg.at[:, 0], 6: quarter,
        7: midg.at[:, 0], 8: gmr, 9: prr, 10: gr1, 11: gfr, 12: gr2, 13: gfz,
        14: gfall.at[:, pl.ds(0, half)], 15: cotg.at[:, 0], 16: midg.at[:, 0],
        17: gmx, 18: prx, 21: quarter, 22: quarter, 24: quarter, 25: quarter, 6: quarter, 20: quarter,
    }
    brings[19] = brings[14]
    leaves = {
        0: small, 1: small, 2: small, 3: small, 5: cotg.at[near, 0], 6: quarter, 7: midg.at[near, 0],
        8: gmr.at[near], 9: prr.at[near], 10: gr1.at[near], 11: filters,
        12: gr2.at[pl.ds(0, nz - 1)], 13: gfz.at[pl.ds(0, nz - 1)], 14: gfall.at[near, pl.ds(0, half)], 15: brings[15], 16: brings[16],
        17: gmx, 18: prx, 19: brings[19], 21: quarter, 22: quarter, 20: quarter, 24: quarter, 25: quarter,
    }

    def arrived(phase):
        wait(brings[phase], recv, phase)

    def left(phase):
        if phase in leaves:
            wait(leaves[phase], send, phase)
        elif phase in (4, 23):

            @pl.when(h != z)
            def _():
                wait(wb.at[0, pl.ds(0, nz)], send, phase)

            @pl.when(h == z)
            def _():
                wait(wb.at[0, pl.ds(0, nz - 1)], send, phase)

    def each(low, high, body):
        def step(k, carry):
            body(k)
            return carry
        lax.fori_loop(low, high, step, 0)

    fetches = []
    for sources in (
        ((tokens_in, tokens),), ((plh_in, plh),), ((pll_in, pll),),
        ((up_in, wts.at[0]),), ((down_in, wts.at[1]),),
        ((cotangent_in, cotangent),), ((mg_in, mg),), ((mt_in, mt),), ((lane_in, lane),),
        ((row_in, row),), ((filter_in.at[:, b], fil.at[0]),), ((filter_out.at[:, b], fil.at[1]),),
    ):
        fetches.append(
            [pltpu.make_async_copy(src, dst, local.at[len(fetches)]) for src, dst in sources]
        )
        for fetch in fetches[-1]:
            fetch.start()

    barrier = pltpu.get_barrier_semaphore()

    def greet(zz, cc):
        pl.semaphore_signal(barrier, inc=1, device_id=(zz, cc), device_id_type=MESH)

    each(1, nc, lambda k: greet(z, lax.rem(c + k, nc)))
    each(0, (nz - 1) * QG, lambda k: greet(lax.rem(z + 1 + k // QG, nz), b * QG + lax.rem(k, QG)))
    each(1, nz, lambda k: greet(lax.rem(z + k, nz), y * nh + z))

    @pl.when(h != z)
    def _():
        each(0, nh, lambda k: greet(h, y * nh + k))

    for phase in (0, 1, 2, 3, 4):
        for fetch in fetches[phase]:
            fetch.wait()
    for i in range(planes):
        toks_t[i * width:(i + 1) * width] = tokens[:, i * plane:(i + 1) * plane]

    def group_out(src, dst, phase):
        def one(k):
            dd = lax.rem(d + STRIDE * k, ng)
            remote(src.at[dd], dst.at[q, z], phase, dd // QG, b * QG + lax.rem(dd, QG))
        each(1, ng, one)
        here(src.at[d], dst.at[q, z], phase)

    def group_back(src, dst, phase):
        def one(k):
            dd = lax.rem(d + STRIDE * k, ng)
            zz, qq = dd // QG, lax.rem(dd, QG)
            remote(src.at[qq, zz], dst.at[d], phase, zz, b * QG + qq)
        each(1, ng, one)
        here(src.at[q, z], dst.at[d], phase)

    def slab_planes(src, dst, phase):
        def one(k):
            cc = lax.rem(c + STRIDE * k, nc)
            part = lax.rem(cc, 2)
            remote(src.at[cc // nh, part], dst.at[c, part], phase, z, cc)
        each(1, nc, one)
        here(src.at[y, core], dst.at[c, core], phase)

    def share(ref, phase):
        remote(ref.at[:, core], ref.at[:, core], phase, z, sibling)

    def slab_parts(src, dst, phase):
        def one(k):
            cc = lax.rem(c + STRIDE * k, nc)
            remote(src.at[cc], dst.at[c], phase, z, cc)
        each(1, nc, one)
        here(src.at[c], dst.at[c], phase)

    def plane_out(parts, dst):
        out = None
        for table, values in parts:
            term = dot(table[...], values, 1, 1)
            out = term if out is None else out + term
        dst[...] = out.astype(bf16).reshape(dst.shape)

    def plane_back(src):
        values = src[...].reshape(ng * comps, LANES)
        return dot(values, plh[...], 0, 0) + dot(values, pll[...], 0, 0)

    first_group = jnp.logical_and(z == 0, q == 0)

    def edge_table():
        return jnp.where(first_group, mt[...], mg[...])

    def evaluate(src):
        rows = nz * comps
        wide = jnp.concatenate([src[k].reshape(rows, LANES) for k in range(QG)], axis=1)
        wide = dot(wide, lane[...]).astype(bf16)
        wide = dot(row[...], wide)
        step = 2 * nz
        lines = jnp.concatenate(
            [
                jnp.concatenate(
                    [wide[k * step:(k + 1) * step, i * LANES:(i + 1) * LANES] for i in range(planes)],
                    axis=0,
                )
                for k in range(cols)
            ],
            axis=1,
        )
        edge = 2 * LANES
        first = dot(edge_table(), lines[:, :edge], precision=HIGHEST)
        rest = dot(mg[...], lines[:, edge:], precision=HIGHEST)
        spec = jnp.concatenate([first, rest], axis=1)
        mids = 2 * nx
        return jnp.concatenate(
            [
                jnp.concatenate(
                    [spec[:mids, k * LANES:(k + 1) * LANES], spec[mids:, k * LANES:(k + 1) * LANES]],
                    axis=1,
                )
                for k in range(cols)
            ],
            axis=0,
        )

    def collect(values, dst):
        mids = 2 * nx
        spec = jnp.concatenate(
            [
                jnp.concatenate(
                    [values[k * mids:(k + 1) * mids, :LANES], values[k * mids:(k + 1) * mids, LANES:]],
                    axis=0,
                )
                for k in range(cols)
            ],
            axis=1,
        )
        edge = 2 * LANES
        first = dot(edge_table(), spec[:, :edge], 0, 0, precision=HIGHEST)
        rest = dot(mg[...], spec[:, edge:], 0, 0, precision=HIGHEST)
        lines = jnp.concatenate([first, rest], axis=1)
        step = 2 * nz
        wide = jnp.concatenate(
            [
                jnp.concatenate(
                    [lines[i * step:(i + 1) * step, k * LANES:(k + 1) * LANES] for i in range(planes)],
                    axis=1,
                )
                for k in range(cols)
            ],
            axis=0,
        ).astype(bf16)
        wide = dot(row[...], wide, 0, 0).astype(bf16)
        wide = dot(wide, lane[...], 1, 1).astype(bf16)
        for k in range(QG):
            dst[k] = wide[:, k * LANES:(k + 1) * LANES].reshape(nz, comps, LANES)

    plane_out([(plh, toks_t[...]), (pll, toks_t[...])], a1s)
    pl.semaphore_wait(
        barrier, nc - 1 + (nz - 1) * QG + nz - 1 + jnp.where(h != z, nh, 0)
    )
    group_out(a1s, a1r, 0)

    wcols = y * nh + z

    def spread(part):
        def one(k):
            zz = lax.rem(z + h + k, nz)
            same = jnp.logical_and(zz == z, h == z)

            @pl.when(jnp.logical_not(same))
            def _():
                remote(wts.at[part], wb.at[part, c], (4, 23)[part], zz, wcols)

            @pl.when(same)
            def _():
                here(wts.at[part], wb.at[part, c], (4, 23)[part])
        each(0, nz, one)

    spread(0)
    spread(1)
    for fetch in fetches[5]:
        fetch.wait()
    for i in range(planes):
        cts[i] = cotangent[:, i * plane:(i + 1) * plane].reshape(2, width // 2, plane)
    slab_planes(cts, cotg, 5)

    for phase in range(6, 12):
        for fetch in fetches[phase]:
            fetch.wait()

    def complex_matrix(k):
        real, imag = fil[k, 0], fil[k, 1]
        return jnp.concatenate(
            [jnp.concatenate([real, imag], axis=1), jnp.concatenate([-imag, real], axis=1)], axis=0
        )

    arrived(0)
    x = evaluate(a1r)
    xs[...] = x
    a = dot(x, complex_matrix(0), precision=HIGHEST)
    as_[...] = a
    collect(dot(gelu(a), complex_matrix(1), precision=HIGHEST), a2s)
    group_back(a2s, a2r, 1)

    after, before = lax.rem(y + 1, ny), lax.rem(y + ny - 1, ny)

    def around(part):
        arrived((4, 23)[part])
        rows = wb.at[part, pl.ds(y * nh, nh)]
        remote(rows, rows, (6, 20)[part], z, after * nh + h)
        remote(rows, rows, (21, 24)[part], z, before * nh + h)

    def onward(part):
        for k, phase, source, to in ((0, (6, 20)[part], before, after), (1, (21, 24)[part], after, before)):
            arrived(phase)
            rows = wb.at[part, pl.ds(source * nh + k * (nh // 2), nh // 2)]
            remote(rows, rows, (22, 25)[part], z, to * nh + h)

    around(0)
    arrived(5)
    share(cotg, 15)

    arrived(1)
    middle = (toks_t[...].astype(f32) + plane_back(a2r)).astype(bf16)
    mid[...] = middle.reshape(mid.shape)
    slab_planes(mid, midg, 7)
    around(1)
    onward(0)
    arrived(7)
    share(midg, 16)

    tile = min(LANES, hidden)
    chans = nc * width

    def hidden_tile(k):
        return pl.ds(pl.multiple_of(k * tile, tile), tile)

    onward(1)
    arrived(15)
    arrived(22)
    arrived(25)

    def back_step(k):
        s = hidden_tile(k)
        back[s, :] = dot(
            wb[1, :, :, s].reshape(chans, tile), cotg[...].reshape(chans, plane), 0, 0
        )
    each(0, hidden // tile, back_step)

    arrived(16)

    def pre_step(k):
        s = hidden_tile(k)
        pre = dot(wb[0, :, :, s].reshape(chans, tile), midg[...].reshape(chans, plane), 0, 0)
        hid[s, :] = gelu(pre).astype(bf16)
        gpre[s, :] = (back[s, :] * gelu_slope(pre)).astype(bf16)
    each(0, hidden // tile, pre_step)

    few = QG

    def shares(weights, values, parts, extra, phase):
        def one(k):
            s = pl.ds(k * few, few)
            part = dot(weights[s].reshape(few * width, hidden), values[...])
            parts[s] = part.astype(bf16).reshape(few, 2, width // 2, plane)
            remote(parts.at[s, other], extra.at[s], phase, z, sibling)
        each(0, nc // few, one)

    def add_pair(parts, extra, total, phase):
        arrived(phase)

        def one(k):
            s = pl.ds(k * few, few)
            total[s] = (parts[s, core].astype(f32) + extra[s].astype(f32)).astype(bf16)
        each(0, nc // few, one)

    def plane_sum(parts, i):
        halves = []
        for k in range(2):
            part = parts[i * nh + k].astype(f32)
            for j in range(k + 2, nh, 2):
                part = part + parts[i * nh + j].astype(f32)
            halves.append(part)
        return jnp.concatenate(halves, axis=0)

    shares(wb.at[0], gpre, gms, gmx, 17)

    def gw_step(k):
        s = pl.ds(k * few, few)
        part = dot(midg[s].reshape(few * width, plane), gpre[...], 1, 1)
        gw[s, 0] = part.astype(bf16).reshape(few, width, hidden)
        part = dot(cotg[s].reshape(few * width, plane), hid[...], 1, 1)
        gw[s, 1] = part.astype(bf16).reshape(few, width, hidden)
    each(0, nc // few, gw_step)

    add_pair(gms, gmx, gmh, 17)
    slab_parts(gmh, gmr, 8)
    shares(wb.at[1], hid, prs, prx, 18)

    arrived(8)
    gm = jnp.concatenate(
        [cts[i].reshape(width, plane).astype(f32) + plane_sum(gmr, i) for i in range(planes)], axis=0
    )
    high, low = split(gm)
    plane_out([(plh, high), (plh, low), (pll, high)], a3s)
    group_out(a3s, a3r, 2)

    add_pair(prs, prx, prh, 18)
    slab_parts(prh, prr, 9)
    slab_parts(gw, gr1, 10)

    arrived(2)
    dy = evaluate(a3r)
    a = as_[...]
    da = dot(dy, complex_matrix(1), 1, 1, precision=HIGHEST) * gelu_slope(a)

    def fold(g):
        return g[:LANES, :LANES] + g[LANES:, LANES:], g[:LANES, LANES:] - g[LANES:, :LANES]

    in_r, in_i = fold(dot(xs[...], da, 0, 0, precision=HIGHEST))
    out_r, out_i = fold(dot(gelu(a), dy, 0, 0, precision=HIGHEST))
    grads = jnp.concatenate([in_r, in_i, out_r, out_i], axis=0)
    gfs[...] = grads.astype(bf16).reshape(gfs.shape)

    group_back(gfs, gfr, 11)
    collect(dot(da, complex_matrix(0), 1, 1, precision=HIGHEST), a4s)
    group_back(a4s, a4r, 3)

    arrived(11)
    part = gfr[0].astype(f32)
    for k in range(1, ng):
        part = part + gfr[k].astype(f32)
    gfp[...] = part.astype(bf16)

    each(1, nz, lambda k: remote(gfp, gfz.at[z], 13, lax.rem(z + k, nz), c))
    here(gfp, gfz.at[z], 13)

    arrived(10)

    def gs_step(k):
        part = gr1[k].astype(f32)
        for i in range(1, ny):
            part = part + gr1[i * nh + k].astype(f32)
        gs[k] = part.astype(bf16)
    each(0, nh, gs_step)

    def gs_out(k):
        zz = lax.rem(z + k, nz)
        remote(gs.at[zz], gr2.at[z], 12, zz, c)
    each(1, nz, gs_out)
    here(gs.at[z], gr2.at[z], 12)

    arrived(13)

    def gf_slab(k):
        cc = lax.rem(c + STRIDE * k, nc)
        own = pl.ds(lax.rem(cc, 2) * half, half)
        remote(gfz.at[own], gfall.at[c, own], 14, z, cc)
    each(1, nc, gf_slab)
    here(gfz.at[pl.ds(core * half, half)], gfall.at[c, pl.ds(core * half, half)], 14)

    arrived(3)
    whole = (gm + plane_back(a4r)).astype(bf16)
    for i in range(planes):
        gtok[:, i * plane:(i + 1) * plane] = whole[i * width:(i + 1) * width]

    arrived(14)
    own = gfall.at[:, pl.ds(core * half, half)]
    remote(own, own, 19, z, sibling)

    arrived(9)
    for i in range(planes):
        whole = mid[i].reshape(width, plane).astype(f32) + plane_sum(prr, i)
        mixed[:, i * plane:(i + 1) * plane] = whole.astype(bf16)

    arrived(12)
    for k, dst in ((0, gup), (1, gdn)):
        part = gr2[0, k].astype(f32)
        for i in range(1, nz):
            part = part + gr2[i, k].astype(f32)
        dst[...] = part

    arrived(19)
    for k in range(nb):
        for j in range(QG):
            (gfi, gfo)[j // 2][j % 2, k] = gfall[k * QG + j].astype(f32).reshape(LANES, LANES)

    for phase in range(26):
        left(phase)


def solution(mesh):
    nz, nc = mesh.shape["tok"], mesh.shape["ch"]

    def local(tokens, filter_in, filter_out, up_weight, down_weight, cotangent):
        rows, width = tokens.shape
        plane = NY * NZ
        planes = rows // plane
        ng = nz * QG
        nb = nc // QG
        nh = nc // planes
        nx = nz * planes
        hidden = up_weight.shape[1]
        comps = plane // ng
        assert nh == nz and planes * width == LANES and QG * width == LANES
        tabs = tables(nz, planes)
        evals = comps // 2 * 2 * nx
        fr = 4 * LANES // ng
        halves = (nc, width // 2, plane)
        block = (nc, 2, width // 2, plane)
        out_shape = (ng, comps, LANES)
        back_shape = (QG, nz, comps, LANES)
        scratch = [
            pltpu.VMEM(shape, bf16)
            for shape in (out_shape, back_shape, back_shape, out_shape) * 2
        ] + [
            pltpu.VMEM((evals, 2 * LANES), f32),
            pltpu.VMEM((evals, 2 * LANES), f32),
            pltpu.VMEM((2, 2, LANES, LANES), f32),
            pltpu.VMEM((LANES, plane), bf16),
            pltpu.VMEM((planes, 2, width // 2, plane), bf16),
            pltpu.VMEM((2, width, hidden), bf16),
            pltpu.VMEM((planes, 2, width // 2, plane), bf16),
            pltpu.VMEM(block, bf16),
            pltpu.VMEM(block, bf16),
            pltpu.VMEM((2, nc, width, hidden), bf16),
            pltpu.VMEM((hidden, plane), f32),
            pltpu.VMEM((hidden, plane), bf16),
            pltpu.VMEM((hidden, plane), bf16),
        ] + [
            pltpu.VMEM(shape, bf16) for shape in (block, halves, halves, halves) * 2
        ] + [
            pltpu.VMEM((nc, 2, width, hidden), bf16),
            pltpu.VMEM((nc, 2, width, hidden), bf16),
            pltpu.VMEM((nh, 2, width, hidden), bf16),
            pltpu.VMEM((nz, 2, width, hidden), bf16),
            pltpu.VMEM((QG, nz, fr, LANES), bf16),
            pltpu.VMEM((ng, fr, LANES), bf16),
            pltpu.VMEM((fr, LANES), bf16),
            pltpu.VMEM((nz, fr, LANES), bf16),
            pltpu.VMEM((nc, nz, fr, LANES), bf16),
            pltpu.VMEM((width, rows), bf16),
            pltpu.VMEM((width, rows), bf16),
            pltpu.VMEM((plane, plane), bf16),
            pltpu.VMEM((plane, plane), bf16),
            pltpu.VMEM((4 * nx, 2 * nx), f32),
            pltpu.VMEM((4 * nx, 2 * nx), f32),
            pltpu.VMEM((QG * LANES, QG * LANES), bf16),
            pltpu.VMEM((nz * comps, nz * comps), bf16),
            pltpu.SemaphoreType.DMA((26,)),
            pltpu.SemaphoreType.DMA((26,)),
            pltpu.SemaphoreType.DMA((12,)),
        ]
        vmem = pl.BlockSpec(memory_space=pltpu.VMEM)
        anywhere = pl.BlockSpec(memory_space=pl.ANY)
        flops = 12 * plane * hidden * nc * width
        mixed, gtok, gup, gdn, gfi, gfo = pl.pallas_call(
            functools.partial(kernel, nz, nc, planes),
            out_shape=(
                jax.ShapeDtypeStruct((width, rows), bf16),
                jax.ShapeDtypeStruct((width, rows), bf16),
                jax.ShapeDtypeStruct((width, hidden), f32),
                jax.ShapeDtypeStruct((width, hidden), f32),
                jax.ShapeDtypeStruct(filter_in.shape, f32),
                jax.ShapeDtypeStruct(filter_out.shape, f32),
            ),
            in_specs=[anywhere] * 12,
            out_specs=[vmem] * 6,
            scratch_shapes=scratch,
            compiler_params=pltpu.CompilerParams(
                collective_id=0, has_side_effects=True, vmem_limit_bytes=60 * 2**20
            ),
            cost_estimate=pl.CostEstimate(flops=flops, bytes_accessed=2**24, transcendentals=2**20),
        )(
            tokens.T, cotangent.T, up_weight, down_weight.T, filter_in, filter_out,
            tabs["high"], tabs["low"], tabs["pair"], tabs["two"], tabs["lane"], tabs["row"],
        )

        return mixed.T, gtok.T, gup, gdn.T, gfi, gfo

    in_specs = (P("tok", "ch"), P(), P(), P("ch", "tok"), P("tok", "ch"), P("tok", "ch"))
    out_specs = (P("tok", "ch"), P("tok", "ch"), P("ch", "tok"), P("tok", "ch"), P(), P())
    return jax.shard_map(local, mesh=mesh, in_specs=in_specs, out_specs=out_specs, check_vma=False)
```

time: 936 us -> 131 us (0.14); the launches traced: 923 us -> 130 us
  waiting for transfers between devices: 513 us -> 0 us
  local copies, waits for them, and re-layouts: 143 us -> 7.32 us
  Pallas kernels: 0 us -> 122 us
  matrix products: 104 us -> 0 us
  starting transfers between devices: 76.8 us -> 0 us
  other arithmetic: 36.4 us -> 0 us
  blocking collectives: 33.9 us -> 0 us
  between operations: 15.3 us -> 0.66 us
    psum x1 -> x0, waiting for transfers between devices: 233 us -> none  [local(): lax.psum((grad_first, grad_second), ('tok', 'ch'))]
    reduce_scatter x4 -> x0, waiting for transfers between devices: 192 us -> none  [the longest x1 87.4 us: local(): lax.psum_scatter(down_term.astype(jnp.bfloat16), 'ch', scatter_dimension=...]
    pallas_call x0 -> x1, Pallas kernels: none -> 122 us  [local(): pl.pallas_call(functools.partial(kernel, nz, nc, planes), out_shape=(jax....]
    dot_general x52 -> x0, matrix products: 94.1 us -> none  [the longest x24 26.5 us: contract(): return jnp.einsum('kqnb,nbd->kqnd', values, matrix, precision=highest)]
    all_to_all x10 -> x0, starting transfers between devices: 75.8 us -> none  [the longest x2 14.9 us: channels_out(): lax.all_to_all(spectrum, 'ch', split_axis=2, concat_axis=3, tiled=True)]
    all_to_all x10 -> x0, waiting for transfers between devices: 64 us -> none  [the longest x2 18.4 us: channels_out(): lax.all_to_all(spectrum, 'ch', split_axis=2, concat_axis=3, tiled=True)]
    unnamed x70 -> x14, local copies, waits for them, and re-layouts: 50.3 us -> 7.32 us
    all_to_all x2 -> x0, blocking collectives: 33.9 us -> none  [the longest x1 20.6 us: lines_back(): lax.all_to_all(spectrum, 'tok', split_axis=1, concat_axis=2, tiled=True)]
  transfers between devices with their start and end apart: 19 -> 0, of which waited for: 12 -> 0; matrix products, arithmetic and copies ran while one was open for 21% -> 0% of each run, Pallas kernels for 0% -> 0%
where the time goes in v1:
time: 131 us; the launch traced here: 130 us
  Pallas kernels  122 us (93%)
  local copies, waits for them, and re-layouts  7.32 us (6%)
    pallas_call x1, Pallas kernels, local(): pl.pallas_call(functools.partial(kernel, nz, nc, planes), out_shape=(jax....  122 us
    unnamed x14, local copies, waits for them, and re-layouts  7.32 us

profile of v1, /device:TPU:1, one launch (start us, length us, event | category | flops | bytes accessed | tf_op | source)
XLA Modules:
  0.0 130.2 jit_solution(15522646041960355847)
XLA Ops:
  0.6 122.3 %shard_map.163 = (bf16[32,2048]{1,0:T(8,128)(2,1)}, bf16[32,2048]{1,0:T(8,128)(2,1)}, f32[32,512]{1,0:T(8,128)}, f32[32,512]{1,0:T(8,128)}, f32[2,8,128,128]{3,2,1,0:T(8,128)}, /*index=5*/f32[2,8,128,128]{3,2,1,0:T(8,128)}) custom-call(bf16[32,2048]{1,0:T(8,128)(2,1)} %bitcast.9, bf16[32,2048]{1,0:T(8,128)(2,1)} %bitcast.10, bf16[32,512]{1,0:T(8,128)(2,1)} %up_in.1, ...), custom_call_target="tpu_custom_call" | custom-call | flops 3221225472 | bytes 16777216 | tf_op jit(solution)/shard_map/pallas_call | solution.py:641
  122.9 0.0 copy-start.1
  122.9 1.6 %copy.24 = bf16[2048,32]{0,1:T(8,128)(2,1)} copy(bf16[2048,32]{0,1:T(8,128)(2,1)} %bitcast.7) | data formatting | bytes 262144
  124.5 0.0 copy-done.1
  124.5 0.0 copy-start.3
  124.5 0.7 copy.25
  125.2 0.2 copy-done.3
  125.4 0.0 copy-start.2
  125.4 0.6 copy.26
  126.0 0.2 copy-done.2
  126.3 0.6 copy.27
  126.9 0.0 copy-start
  126.9 2.4 %copy.28 = f32[2,8,128,128]{3,2,1,0:T(8,128)} copy(f32[2,8,128,128]{3,2,1,0:T(8,128)} %get-tuple-element.28) | data formatting | bytes 2097152
  129.3 0.0 copy-done
  129.3 1.0 copy.29
Async XLA Ops:
  122.9 1.6 %copy-start.1 = (bf16[32,2048]{1,0:T(8,128)(2,1)S(1)}, bf16[32,2048]{1,0:T(8,128)(2,1)}, u32[]{:S(2)}) copy-start(bf16[32,2048]{1,0:T(8,128)(2,1)} %get-tuple-element.13) | copy-start | bytes 393220
  124.5 0.9 copy-start.3
  125.4 0.9 copy-start.2
  126.9 2.4 %copy-start = (f32[2,8,128,128]{3,2,1,0:T(8,128)S(1)}, f32[2,8,128,128]{3,2,1,0:T(8,128)}, u32[]{:S(2)}) copy-start(f32[2,8,128,128]{3,2,1,0:T(8,128)} %get-tuple-element.29) | copy-start | bytes 3145732

commit v2 on v1

--- a/solution.py
+++ b/solution.py
@@ -90,6 +90,16 @@
     )
 
 
+def split(x):
+    high = x.astype(bf16)
+    return high, (x - high.astype(f32)).astype(bf16)
+
+
+def dot3(a, b, ca=1, cb=0):
+    (ah, al), (bh, bl) = split(a), split(b)
+    return dot(ah, bh, ca, cb) + (dot(ah, bl, ca, cb) + dot(al, bh, ca, cb))
+
+
 SCALE = math.sqrt(2.0 / math.pi)
 CUBIC = 0.044715
 
@@ -102,11 +112,6 @@
 def gelu_slope(x):
     t = jnp.tanh(SCALE * (x + CUBIC * (x * x * x)))
     return 0.5 * (1.0 + t) + 0.5 * x * (1.0 - t * t) * (SCALE * (1.0 + 3.0 * CUBIC * (x * x)))
-
-
-def split(x):
-    high = x.astype(bf16)
-    return high, (x - high.astype(f32)).astype(bf16)
 
 
 def kernel(
@@ -159,15 +164,15 @@
     half = nz // 2
     brings = {
         0: a1r, 1: a2r, 2: a3r, 3: a4r, 4: quarter, 23: quarter, 5: cotg.at[:, 0], 6: quarter,
-        7: midg.at[:, 0], 8: gmr, 9: prr, 10: gr1, 11: gfr, 12: gr2, 13: gfz,
+        7: midg.at[:, 0], 8: gmr, 9: prr, 10: gr1.at[0], 26: gr1.at[0], 11: gfr, 12: gr2.at[0], 27: gr2.at[0], 13: gfz,
         14: gfall.at[:, pl.ds(0, half)], 15: cotg.at[:, 0], 16: midg.at[:, 0],
         17: gmx, 18: prx, 21: quarter, 22: quarter, 24: quarter, 25: quarter, 6: quarter, 20: quarter,
     }
     brings[19] = brings[14]
     leaves = {
         0: small, 1: small, 2: small, 3: small, 5: cotg.at[near, 0], 6: quarter, 7: midg.at[near, 0],
-        8: gmr.at[near], 9: prr.at[near], 10: gr1.at[near], 11: filters,
-        12: gr2.at[pl.ds(0, nz - 1)], 13: gfz.at[pl.ds(0, nz - 1)], 14: gfall.at[near, pl.ds(0, half)], 15: brings[15], 16: brings[16],
+        8: gmr.at[near], 9: prr.at[near], 10: gr1.at[0, near], 26: gr1.at[0, near], 11: filters,
+        12: gr2.at[0, pl.ds(0, nz - 1)], 27: gr2.at[0, pl.ds(0, nz - 1)], 13: gfz.at[pl.ds(0, nz - 1)], 14: gfall.at[near, pl.ds(0, half)], 15: brings[15], 16: brings[16],
         17: gmx, 18: prx, 19: brings[19], 21: quarter, 22: quarter, 20: quarter, 24: quarter, 25: quarter,
     }
 
@@ -381,9 +386,9 @@
     arrived(0)
     x = evaluate(a1r)
     xs[...] = x
-    a = dot(x, complex_matrix(0), precision=HIGHEST)
+    a = dot3(x, complex_matrix(0))
     as_[...] = a
-    collect(dot(gelu(a), complex_matrix(1), precision=HIGHEST), a2s)
+    collect(dot3(gelu(a), complex_matrix(1)), a2s)
     group_back(a2s, a2r, 1)
 
     after, before = lax.rem(y + 1, ny), lax.rem(y + ny - 1, ny)
@@ -472,14 +477,31 @@
     def gw_step(k):
         s = pl.ds(k * few, few)
         part = dot(midg[s].reshape(few * width, plane), gpre[...], 1, 1)
-        gw[s, 0] = part.astype(bf16).reshape(few, width, hidden)
+        gw[0, s] = part.astype(bf16).reshape(few, width, hidden)
         part = dot(cotg[s].reshape(few * width, plane), hid[...], 1, 1)
-        gw[s, 1] = part.astype(bf16).reshape(few, width, hidden)
+        gw[1, s] = part.astype(bf16).reshape(few, width, hidden)
     each(0, nc // few, gw_step)
 
     add_pair(gms, gmx, gmh, 17)
     slab_parts(gmh, gmr, 8)
+    slab_parts(gw.at[0], gr1.at[0], 10)
     shares(wb.at[1], hid, prs, prx, 18)
+
+    def weight_sums(part):
+        arrived((10, 26)[part])
+
+        def one(k):
+            total = gr1[part, k].astype(f32)
+            for i in range(1, ny):
+                total = total + gr1[part, i * nh + k].astype(f32)
+            gs[part, k] = total.astype(bf16)
+        each(0, nh, one)
+
+        def out(k):
+            zz = lax.rem(z + k, nz)
+            remote(gs.at[part, zz], gr2.at[part, z], (12, 27)[part], zz, c)
+        each(1, nz, out)
+        here(gs.at[part, z], gr2.at[part, z], (12, 27)[part])
 
     arrived(8)
     gm = jnp.concatenate(
@@ -489,26 +511,27 @@
     plane_out([(plh, high), (plh, low), (pll, high)], a3s)
     group_out(a3s, a3r, 2)
 
-    add_pair(prs, prx, prh, 18)
-    slab_parts(prh, prr, 9)
-    slab_parts(gw, gr1, 10)
+    slab_parts(gw.at[1], gr1.at[1], 26)
 
     arrived(2)
     dy = evaluate(a3r)
     a = as_[...]
-    da = dot(dy, complex_matrix(1), 1, 1, precision=HIGHEST) * gelu_slope(a)
+    da = dot3(dy, complex_matrix(1), 1, 1) * gelu_slope(a)
 
     def fold(g):
         return g[:LANES, :LANES] + g[LANES:, LANES:], g[:LANES, LANES:] - g[LANES:, :LANES]
 
-    in_r, in_i = fold(dot(xs[...], da, 0, 0, precision=HIGHEST))
-    out_r, out_i = fold(dot(gelu(a), dy, 0, 0, precision=HIGHEST))
+    in_r, in_i = fold(dot3(xs[...], da, 0, 0))
+    out_r, out_i = fold(dot3(gelu(a), dy, 0, 0))
     grads = jnp.concatenate([in_r, in_i, out_r, out_i], axis=0)
     gfs[...] = grads.astype(bf16).reshape(gfs.shape)
 
     group_back(gfs, gfr, 11)
-    collect(dot(da, complex_matrix(0), 1, 1, precision=HIGHEST), a4s)
+    collect(dot3(da, complex_matrix(0), 1, 1), a4s)
     group_back(a4s, a4r, 3)
+    weight_sums(0)
+    add_pair(prs, prx, prh, 18)
+    slab_parts(prh, prr, 9)
 
     arrived(11)
     part = gfr[0].astype(f32)
@@ -519,20 +542,7 @@
     each(1, nz, lambda k: remote(gfp, gfz.at[z], 13, lax.rem(z + k, nz), c))
     here(gfp, gfz.at[z], 13)
 
-    arrived(10)
-
-    def gs_step(k):
-        part = gr1[k].astype(f32)
-        for i in range(1, ny):
-            part = part + gr1[i * nh + k].astype(f32)
-        gs[k] = part.astype(bf16)
-    each(0, nh, gs_step)
-
-    def gs_out(k):
-        zz = lax.rem(z + k, nz)
-        remote(gs.at[zz], gr2.at[z], 12, zz, c)
-    each(1, nz, gs_out)
-    here(gs.at[z], gr2.at[z], 12)
+    weight_sums(1)
 
     arrived(13)
 
@@ -557,11 +567,11 @@
         whole = mid[i].reshape(width, plane).astype(f32) + plane_sum(prr, i)
         mixed[:, i * plane:(i + 1) * plane] = whole.astype(bf16)
 
-    arrived(12)
     for k, dst in ((0, gup), (1, gdn)):
-        part = gr2[0, k].astype(f32)
+        arrived((12, 27)[k])
+        part = gr2[k, 0].astype(f32)
         for i in range(1, nz):
-            part = part + gr2[i, k].astype(f32)
+            part = part + gr2[k, i].astype(f32)
         dst[...] = part
 
     arrived(19)
@@ -569,7 +579,7 @@
         for j in range(QG):
             (gfi, gfo)[j // 2][j % 2, k] = gfall[k * QG + j].astype(f32).reshape(LANES, LANES)
 
-    for phase in range(26):
+    for phase in range(28):
         left(phase)
 
 
@@ -614,10 +624,10 @@
         ] + [
             pltpu.VMEM(shape, bf16) for shape in (block, halves, halves, halves) * 2
         ] + [
-            pltpu.VMEM((nc, 2, width, hidden), bf16),
-            pltpu.VMEM((nc, 2, width, hidden), bf16),
-            pltpu.VMEM((nh, 2, width, hidden), bf16),
-            pltpu.VMEM((nz, 2, width, hidden), bf16),
+            pltpu.VMEM((2, nc, width, hidden), bf16),
+            pltpu.VMEM((2, nc, width, hidden), bf16),
+            pltpu.VMEM((2, nh, width, hidden), bf16),
+            pltpu.VMEM((2, nz, width, hidden), bf16),
             pltpu.VMEM((QG, nz, fr, LANES), bf16),
             pltpu.VMEM((ng, fr, LANES), bf16),
             pltpu.VMEM((fr, LANES), bf16),
@@ -631,8 +641,8 @@
             pltpu.VMEM((4 * nx, 2 * nx), f32),
             pltpu.VMEM((QG * LANES, QG * LANES), bf16),
             pltpu.VMEM((nz * comps, nz * comps), bf16),
-            pltpu.SemaphoreType.DMA((26,)),
-            pltpu.SemaphoreType.DMA((26,)),
+            pltpu.SemaphoreType.DMA((28,)),
+            pltpu.SemaphoreType.DMA((28,)),
             pltpu.SemaphoreType.DMA((12,)),
         ]
         vmem = pl.BlockSpec(memory_space=pltpu.VMEM)

time: 131 us -> 122 us (0.931)
  Pallas kernels: 122 us -> 113 us
    pallas_call x1, Pallas kernels: 122 us -> 113 us  [local(): pl.pallas_call(functools.partial(kernel, nz, nc, planes), out_shape=(jax....]
where the time goes in v2:
time: 122 us; the launch traced here: 121 us
  Pallas kernels  113 us (93%)
  local copies, waits for them, and re-layouts  7.32 us (6%)
    pallas_call x1, Pallas kernels, local(): pl.pallas_call(functools.partial(kernel, nz, nc, planes), out_shape=(jax....  113 us
    unnamed x14, local copies, waits for them, and re-layouts  7.32 us

profile of v2, /device:TPU:1, one launch (start us, length us, event | category | flops | bytes accessed | tf_op | source)
XLA Modules:
  0.0 121.5 jit_solution(10735841421939925535)
XLA Ops:
  0.6 113.5 %shard_map.163 = (bf16[32,2048]{1,0:T(8,128)(2,1)}, bf16[32,2048]{1,0:T(8,128)(2,1)}, f32[32,512]{1,0:T(8,128)}, f32[32,512]{1,0:T(8,128)}, f32[2,8,128,128]{3,2,1,0:T(8,128)}, /*index=5*/f32[2,8,128,128]{3,2,1,0:T(8,128)}) custom-call(bf16[32,2048]{1,0:T(8,128)(2,1)} %bitcast.9, bf16[32,2048]{1,0:T(8,128)(2,1)} %bitcast.10, bf16[32,512]{1,0:T(8,128)(2,1)} %up_in.1, ...), custom_call_target="tpu_custom_call" | custom-call | flops 3221225472 | bytes 16777216 | tf_op jit(solution)/shard_map/pallas_call | solution.py:651
  114.1 0.0 copy-start.1
  114.1 1.6 %copy.24 = bf16[2048,32]{0,1:T(8,128)(2,1)} copy(bf16[2048,32]{0,1:T(8,128)(2,1)} %bitcast.7) | data formatting | bytes 262144
  115.7 0.0 copy-done.1
  115.7 0.0 copy-start.3
  115.7 0.7 copy.25
  116.4 0.2 copy-done.3
  116.6 0.0 copy-start.2
  116.6 0.6 copy.26
  117.2 0.2 copy-done.2
  117.5 0.6 copy.27
  118.1 0.0 copy-start
  118.1 2.4 %copy.28 = f32[2,8,128,128]{3,2,1,0:T(8,128)} copy(f32[2,8,128,128]{3,2,1,0:T(8,128)} %get-tuple-element.28) | data formatting | bytes 2097152
  120.5 0.0 copy-done
  120.5 1.0 copy.29
Async XLA Ops:
  114.1 1.6 %copy-start.1 = (bf16[32,2048]{1,0:T(8,128)(2,1)S(1)}, bf16[32,2048]{1,0:T(8,128)(2,1)}, u32[]{:S(2)}) copy-start(bf16[32,2048]{1,0:T(8,128)(2,1)} %get-tuple-element.13) | copy-start | bytes 393220
  115.7 0.9 copy-start.3
  116.6 0.9 copy-start.2
  118.1 2.4 %copy-start = (f32[2,8,128,128]{3,2,1,0:T(8,128)S(1)}, f32[2,8,128,128]{3,2,1,0:T(8,128)}, u32[]{:S(2)}) copy-start(f32[2,8,128,128]{3,2,1,0:T(8,128)} %get-tuple-element.29) | copy-start | bytes 3145732

commit v3 on v2

--- a/solution.py
+++ b/solution.py
@@ -542,7 +542,10 @@
     each(1, nz, lambda k: remote(gfp, gfz.at[z], 13, lax.rem(z + k, nz), c))
     here(gfp, gfz.at[z], 13)
 
-    weight_sums(1)
+    arrived(3)
+    whole = (gm + plane_back(a4r)).astype(bf16)
+    for i in range(planes):
+        gtok[:, i * plane:(i + 1) * plane] = whole[i * width:(i + 1) * width]
 
     arrived(13)
 
@@ -552,11 +555,8 @@
         remote(gfz.at[own], gfall.at[c, own], 14, z, cc)
     each(1, nc, gf_slab)
     here(gfz.at[pl.ds(core * half, half)], gfall.at[c, pl.ds(core * half, half)], 14)
-
-    arrived(3)
-    whole = (gm + plane_back(a4r)).astype(bf16)
-    for i in range(planes):
-        gtok[:, i * plane:(i + 1) * plane] = whole[i * width:(i + 1) * width]
+    weight_sums(1)
+
 
     arrived(14)
     own = gfall.at[:, pl.ds(core * half, half)]

time: 122 us -> 122 us (level)
  no operation moved by 1% of the time
where the time goes in v3:
time: 122 us
  Pallas kernels  114 us (93%)
  local copies, waits for them, and re-layouts  7.32 us (6%)
    pallas_call x1, Pallas kernels, local(): pl.pallas_call(functools.partial(kernel, nz, nc, planes), out_shape=(jax....  114 us
    unnamed x14, local copies, waits for them, and re-layouts  7.32 us

profile of v3, /device:TPU:1, one launch (start us, length us, event | category | flops | bytes accessed | tf_op | source)
XLA Modules:
  0.0 121.6 jit_solution(16455261870056033116)
XLA Ops:
  0.6 113.7 %shard_map.163 = (bf16[32,2048]{1,0:T(8,128)(2,1)}, bf16[32,2048]{1,0:T(8,128)(2,1)}, f32[32,512]{1,0:T(8,128)}, f32[32,512]{1,0:T(8,128)}, f32[2,8,128,128]{3,2,1,0:T(8,128)}, /*index=5*/f32[2,8,128,128]{3,2,1,0:T(8,128)}) custom-call(bf16[32,2048]{1,0:T(8,128)(2,1)} %bitcast.9, bf16[32,2048]{1,0:T(8,128)(2,1)} %bitcast.10, bf16[32,512]{1,0:T(8,128)(2,1)} %up_in.1, ...), custom_call_target="tpu_custom_call" | custom-call | flops 3221225472 | bytes 16777216 | tf_op jit(solution)/shard_map/pallas_call | solution.py:651
  114.3 0.0 copy-start.1
  114.3 1.6 %copy.24 = bf16[2048,32]{0,1:T(8,128)(2,1)} copy(bf16[2048,32]{0,1:T(8,128)(2,1)} %bitcast.7) | data formatting | bytes 262144
  115.9 0.0 copy-done.1
  115.9 0.0 copy-start.3
  115.9 0.7 copy.25
  116.6 0.2 copy-done.3
  116.8 0.0 copy-start.2
  116.8 0.6 copy.26
  117.4 0.2 copy-done.2
  117.6 0.6 copy.27
  118.3 0.0 copy-start
  118.3 2.4 %copy.28 = f32[2,8,128,128]{3,2,1,0:T(8,128)} copy(f32[2,8,128,128]{3,2,1,0:T(8,128)} %get-tuple-element.28) | data formatting | bytes 2097152
  120.7 0.0 copy-done
  120.7 1.0 copy.29
Async XLA Ops:
  114.3 1.6 %copy-start.1 = (bf16[32,2048]{1,0:T(8,128)(2,1)S(1)}, bf16[32,2048]{1,0:T(8,128)(2,1)}, u32[]{:S(2)}) copy-start(bf16[32,2048]{1,0:T(8,128)(2,1)} %get-tuple-element.13) | copy-start | bytes 393220
  115.9 0.9 copy-start.3
  116.8 0.9 copy-start.2
  118.3 2.4 %copy-start = (f32[2,8,128,128]{3,2,1,0:T(8,128)S(1)}, f32[2,8,128,128]{3,2,1,0:T(8,128)}, u32[]{:S(2)}) copy-start(f32[2,8,128,128]{3,2,1,0:T(8,128)} %get-tuple-element.29) | copy-start | bytes 3145732

commit v4 on v3

--- a/solution.py
+++ b/solution.py
@@ -474,17 +474,17 @@
 
     shares(wb.at[0], gpre, gms, gmx, 17)
 
-    def gw_step(k):
-        s = pl.ds(k * few, few)
-        part = dot(midg[s].reshape(few * width, plane), gpre[...], 1, 1)
-        gw[0, s] = part.astype(bf16).reshape(few, width, hidden)
-        part = dot(cotg[s].reshape(few * width, plane), hid[...], 1, 1)
-        gw[1, s] = part.astype(bf16).reshape(few, width, hidden)
-    each(0, nc // few, gw_step)
+    def weight_terms(part, left_side, right_side):
+        def one(k):
+            s = pl.ds(k * few, few)
+            term = dot(left_side[s].reshape(few * width, plane), right_side[...], 1, 1)
+            gw[part, s] = term.astype(bf16).reshape(few, width, hidden)
+        each(0, nc // few, one)
+        slab_parts(gw.at[part], gr1.at[part], (10, 26)[part])
 
     add_pair(gms, gmx, gmh, 17)
     slab_parts(gmh, gmr, 8)
-    slab_parts(gw.at[0], gr1.at[0], 10)
+    weight_terms(0, midg, gpre)
     shares(wb.at[1], hid, prs, prx, 18)
 
     def weight_sums(part):
@@ -511,7 +511,7 @@
     plane_out([(plh, high), (plh, low), (pll, high)], a3s)
     group_out(a3s, a3r, 2)
 
-    slab_parts(gw.at[1], gr1.at[1], 26)
+    weight_terms(1, cotg, hid)
 
     arrived(2)
     dy = evaluate(a3r)

time: 122 us -> 118 us (0.967)
  Pallas kernels: 114 us -> 110 us
    pallas_call x1, Pallas kernels: 114 us -> 110 us  [local(): pl.pallas_call(functools.partial(kernel, nz, nc, planes), out_shape=(jax....]
where the time goes in v4:
time: 118 us
  Pallas kernels  110 us (93%)
  local copies, waits for them, and re-layouts  7.32 us (6%)
    pallas_call x1, Pallas kernels, local(): pl.pallas_call(functools.partial(kernel, nz, nc, planes), out_shape=(jax....  110 us
    unnamed x14, local copies, waits for them, and re-layouts  7.32 us

profile of v4, /device:TPU:1, one launch (start us, length us, event | category | flops | bytes accessed | tf_op | source)
XLA Modules:
  0.0 117.8 jit_solution(11926773877850122141)
XLA Ops:
  0.6 109.8 %shard_map.163 = (bf16[32,2048]{1,0:T(8,128)(2,1)}, bf16[32,2048]{1,0:T(8,128)(2,1)}, f32[32,512]{1,0:T(8,128)}, f32[32,512]{1,0:T(8,128)}, f32[2,8,128,128]{3,2,1,0:T(8,128)}, /*index=5*/f32[2,8,128,128]{3,2,1,0:T(8,128)}) custom-call(bf16[32,2048]{1,0:T(8,128)(2,1)} %bitcast.9, bf16[32,2048]{1,0:T(8,128)(2,1)} %bitcast.10, bf16[32,512]{1,0:T(8,128)(2,1)} %up_in.1, ...), custom_call_target="tpu_custom_call" | custom-call | flops 3221225472 | bytes 16777216 | tf_op jit(solution)/shard_map/pallas_call | solution.py:651
  110.5 0.0 copy-start.1
  110.5 1.6 %copy.24 = bf16[2048,32]{0,1:T(8,128)(2,1)} copy(bf16[2048,32]{0,1:T(8,128)(2,1)} %bitcast.7) | data formatting | bytes 262144
  112.1 0.0 copy-done.1
  112.1 0.0 copy-start.3
  112.1 0.7 copy.25
  112.7 0.2 copy-done.3
  112.9 0.0 copy-start.2
  112.9 0.6 copy.26
  113.6 0.2 copy-done.2
  113.8 0.6 copy.27
  114.4 0.0 copy-start
  114.4 2.4 %copy.28 = f32[2,8,128,128]{3,2,1,0:T(8,128)} copy(f32[2,8,128,128]{3,2,1,0:T(8,128)} %get-tuple-element.28) | data formatting | bytes 2097152
  116.8 0.0 copy-done
  116.8 1.0 copy.29
Async XLA Ops:
  110.5 1.6 %copy-start.1 = (bf16[32,2048]{1,0:T(8,128)(2,1)S(1)}, bf16[32,2048]{1,0:T(8,128)(2,1)}, u32[]{:S(2)}) copy-start(bf16[32,2048]{1,0:T(8,128)(2,1)} %get-tuple-element.13) | copy-start | bytes 393220
  112.1 0.9 copy-start.3
  112.9 0.9 copy-start.2
  114.4 2.4 %copy-start = (f32[2,8,128,128]{3,2,1,0:T(8,128)S(1)}, f32[2,8,128,128]{3,2,1,0:T(8,128)}, u32[]{:S(2)}) copy-start(f32[2,8,128,128]{3,2,1,0:T(8,128)} %get-tuple-element.29) | copy-start | bytes 3145732
